TPU v7x, 512 devices: a whole 4x8x8 slice. The times are simulated.
512 devices in a mesh: row: 16 (over y, core), col: 32 (over x, z).
Axes of the slice: x: 4, y: 8, z: 8, core: 2. Of those that a mesh axis runs over, the one named last changes fastest.
Arguments:
- tokens: bfloat16 [2304, 8192], P('col', 'row'), may hold values from -6 to 6
- out_grad: bfloat16 [2304, 8192], P('col', 'row'), may hold values from -6 to 6
- gate_pre: bfloat16 [2304, 12288], P('row', 'col'), may hold values from -8 to 8
- up_pre: bfloat16 [2304, 12288], P('row', 'col'), may hold values from -6 to 6
- w_gate: bfloat16 [8192, 12288], P('row', 'col'), may hold values from -0.0625 to 0.0625
- w_up: bfloat16 [8192, 12288], P('row', 'col'), may hold values from -0.0625 to 0.0625
- w_down: bfloat16 [12288, 8192], P('col', 'row'), may hold values from -0.0546875 to 0.0546875
Outputs:
- token_grad: bfloat16 [2304, 8192], P('col', 'row')
- gate_wgrad: bfloat16 [8192, 12288], P('row', 'col')
- up_wgrad: bfloat16 [8192, 12288], P('row', 'col')
- down_wgrad: bfloat16 [12288, 8192], P('col', 'row')
All inputs are finite; a program needn't handle non-finite values.
Results may differ from a plain program's by a relative error of at most 0.035.
Values may be sent and summed in bfloat16 or wider, within the bound.
No kernel may reach another device: no remote copies, remote signals or barrier semaphores. Data moves between devices by JAX's collectives and lax.ppermute only.
A program may use at most 64 MiB of HBM per device.

v0:
```python
import jax
import jax.numpy as jnp
from jax import lax
from jax.sharding import PartitionSpec as P


def contract_last(left_side, right_side):
    return lax.dot_general(
        left_side, right_side, (((1,), (1,)), ((), ())), preferred_element_type=jnp.float32
    )


def contract_first(left_side, right_side):
    return lax.dot_general(
        left_side, right_side, (((0,), (0,)), ((), ())), preferred_element_type=jnp.float32
    )


def swiglu_grads(hidden_grad, gate_pre, up_pre):
    gate_float = gate_pre.astype(jnp.float32)
    up_float = up_pre.astype(jnp.float32)
    sigmoid_gate = jax.nn.sigmoid(gate_float)
    swish_gate = gate_float * sigmoid_gate
    gate_grad = (
        hidden_grad * up_float * sigmoid_gate * (1.0 + gate_float * (1.0 - sigmoid_gate))
    ).astype(jnp.bfloat16)
    up_grad = (hidden_grad * swish_gate).astype(jnp.bfloat16)
    hidden = (swish_gate * up_float).astype(jnp.bfloat16)
    return (gate_grad, up_grad, hidden)


def local(tokens, out_grad, gate_pre, up_pre, w_gate, w_up, w_down):
    token_rows, grad_rows = (
        lax.all_gather(tokens, "col", axis=0, tiled=True),
        lax.all_gather(out_grad, "col", axis=0, tiled=True),
    )
    total_rows = grad_rows.shape[0]
    hidden_grad = lax.psum_scatter(
        contract_last(grad_rows, w_down).astype(jnp.bfloat16),
        "row",
        scatter_dimension=0,
        tiled=True,
    ).astype(jnp.float32)
    gate_share, up_share, hidden_share = swiglu_grads(hidden_grad, gate_pre, up_pre)
    gate_grad, up_grad, hidden = (
        lax.all_gather(gate_share, "row", axis=0, tiled=True),
        lax.all_gather(up_share, "row", axis=0, tiled=True),
        lax.all_gather(hidden_share, "row", axis=0, tiled=True),
    )
    token_grad = lax.psum_scatter(
        (contract_last(gate_grad, w_gate) + contract_last(up_grad, w_up)).astype(jnp.bfloat16),
        "col",
        scatter_dimension=0,
        tiled=True,
    )
    grad_scale = total_rows ** (-0.5)
    gate_wgrad = (contract_first(token_rows, gate_grad) * grad_scale).astype(jnp.bfloat16)
    up_wgrad = (contract_first(token_rows, up_grad) * grad_scale).astype(jnp.bfloat16)
    down_wgrad = (contract_first(hidden, grad_rows) * grad_scale).astype(jnp.bfloat16)
    return (token_grad, gate_wgrad, up_wgrad, down_wgrad)


def solution(mesh):
    return jax.shard_map(
        local,
        mesh=mesh,
        in_specs=(
            P("col", "row"),
            P("col", "row"),
            P("row", "col"),
            P("row", "col"),
            P("row", "col"),
            P("row", "col"),
            P("col", "row"),
        ),
        out_specs=(P("col", "row"), P("row", "col"), P("row", "col"), P("col", "row")),
        check_vma=False,
    )
```

profile of v0, /device:TPU:16, one launch (start us, length us, event | category | flops | bytes accessed | tf_op | source)
XLA Modules:
  0.0 613.3 jit_solution(11523516848758164644)
XLA Ops:
  7.2 0.0 copy-start
  7.2 0.0 all-gather.6.cloned.1.call-start
  7.2 0.7 all-gather.6.cloned.1.call-update
  7.9 0.0 reduce-scatter.3.cloned.1.call-start
  8.0 92.0 %all-gather.6.cloned.1.call-done = bf16[2304,512]{1,0:T(8,128)(2,1)} async-done(((bf16[72,512]{1,0:T(8,128)(2,1)}), bf16[2304,512]{1,0:T(8,128)(2,1)}) %all-gather.6.cloned.1.call-update) | async-done | bytes 2359312 | tf_op jit(solution)/shard_map/all_gather | solution.py:35
  99.9 4.4 convolution_convert_fusion
  104.3 0.0 reduce-scatter.3.cloned.1.call-update
  104.3 0.0 all-gather.8.cloned.1.call-start
  104.4 53.0 %reduce-scatter.3.cloned.1.call-done = bf16[144,384]{1,0:T(8,128)(2,1)} async-done(((bf16[2304,384]{1,0:T(8,128)(2,1)}), bf16[144,384]{1,0:T(8,128)(2,1)}) %reduce-scatter.3.cloned.1.call-update) | async-done | bytes 110608 | tf_op jit(solution)/shard_map/reduce_scatter | solution.py:38
  157.4 1.7 fusion.10
  159.1 0.0 all-gather.8.cloned.1.call-update
  159.2 0.0 all-gather.10.cloned.1.call-start
  159.2 0.5 all-gather.10.cloned.1.call-update
  159.7 0.0 all-gather.12.cloned.1.call-start
  159.8 0.5 all-gather.12.cloned.1.call-update
  160.3 0.0 all-gather.14.cloned.1.call-start
  160.4 0.5 all-gather.14.cloned.1.call-update
  160.9 0.0 copy-start.2
  160.9 0.0 reduce-scatter.5.cloned.1.call-start
  161.0 43.9 %all-gather.8.cloned.1.call-done = bf16[2304,384]{1,0:T(8,128)(2,1)} async-done(((bf16[144,384]{1,0:T(8,128)(2,1)}), bf16[2304,384]{1,0:T(8,128)(2,1)}) %all-gather.8.cloned.1.call-update) | async-done | bytes 1769488 | tf_op jit(solution)/shard_map/all_gather | solution.py:46
  204.9 5.0 fusion.15
  209.9 38.3 %all-gather.10.cloned.1.call-done = bf16[2304,384]{1,0:T(8,128)(2,1)} async-done(((bf16[144,384]{1,0:T(8,128)(2,1)}), bf16[2304,384]{1,0:T(8,128)(2,1)}) %all-gather.10.cloned.1.call-update) | async-done | bytes 1769488 | tf_op jit(solution)/shard_map/all_gather | solution.py:47
  248.2 5.7 fusion
  253.9 0.0 reduce-scatter.5.cloned.1.call-update
  253.9 82.2 %all-gather.12.cloned.1.call-done = bf16[2304,512]{1,0:T(8,128)(2,1)} async-done(((bf16[72,512]{1,0:T(8,128)(2,1)}), bf16[2304,512]{1,0:T(8,128)(2,1)}) %all-gather.12.cloned.1.call-update) | async-done | bytes 2359312 | tf_op jit(solution)/shard_map/all_gather | solution.py:34
  336.1 2.8 fusion.5
  338.9 0.9 copy.11
  339.8 3.5 fusion.4
  343.3 0.9 copy.12
  344.2 32.2 %all-gather.14.cloned.1.call-done = bf16[2304,384]{1,0:T(8,128)(2,1)} async-done(((bf16[144,384]{1,0:T(8,128)(2,1)}), bf16[2304,384]{1,0:T(8,128)(2,1)}) %all-gather.14.cloned.1.call-update) | async-done | bytes 1769488 | tf_op jit(solution)/shard_map/all_gather | solution.py:48
  376.3 3.3 fusion.3
  379.7 226.8 %reduce-scatter.5.cloned.1.call-done = bf16[72,512]{1,0:T(8,128)(2,1)} async-done(((bf16[2304,512]{1,0:T(8,128)(2,1)}), bf16[72,512]{1,0:T(8,128)(2,1)}) %reduce-scatter.5.cloned.1.call-update) | async-done | bytes 73744 | tf_op jit(solution)/shard_map/reduce_scatter | solution.py:50
  (10 shorter events, 0.0 us)
Async XLA Ops:
  7.2 197.7 %copy-start = (bf16[512,384]{1,0:T(8,128)(2,1)S(1)}, bf16[512,384]{1,0:T(8,128)(2,1)}, u32[]{:S(2)}) copy-start(bf16[512,384]{1,0:T(8,128)(2,1)} %param.11) | copy-start | bytes 1179652
  7.2 92.8 %all-gather.6.cloned.1.call-start = ((), (), s32[]{:S(2)}) async-start(), calls=%async_computation.2 | async-start | bytes 2433024 | tf_op jit(solution)/shard_map/all_gather | solution.py:35
  7.9 149.5 %copy-start.3 = (bf16[144,384]{1,0:T(8,128)(2,1)S(1)}, bf16[144,384]{1,0:T(8,128)(2,1)}, u32[]{:S(2)}) copy-start(bf16[144,384]{1,0:T(8,128)(2,1)} %param.10) | copy-start | bytes 331780
  7.9 149.5 %copy-start.4 = (bf16[144,384]{1,0:T(8,128)(2,1)S(1)}, bf16[144,384]{1,0:T(8,128)(2,1)}, u32[]{:S(2)}) copy-start(bf16[144,384]{1,0:T(8,128)(2,1)} %param.9) | copy-start | bytes 331780
  7.9 149.4 %reduce-scatter.3.cloned.1.call-start = ((), (), s32[]{:S(2)}) async-start(), calls=%async_computation.3 | async-start | bytes 1880064 | tf_op jit(solution)/shard_map/reduce_scatter | solution.py:38
  104.3 100.5 %all-gather.8.cloned.1.call-start = ((), (), s32[]{:S(2)}) async-start(), calls=%async_computation.4 | async-start | bytes 1880064 | tf_op jit(solution)/shard_map/all_gather | solution.py:46
  159.2 89.1 %all-gather.10.cloned.1.call-start = ((), (), s32[]{:S(2)}) async-start(), calls=%async_computation.5 | async-start | bytes 1880064 | tf_op jit(solution)/shard_map/all_gather | solution.py:47
  159.7 176.4 %all-gather.12.cloned.1.call-start = ((), (), s32[]{:S(2)}) async-start(), calls=%async_computation.7 | async-start | bytes 2433024 | tf_op jit(solution)/shard_map/all_gather | solution.py:34
  160.3 216.0 %all-gather.14.cloned.1.call-start = ((), (), s32[]{:S(2)}) async-start(), calls=%async_computation.8 | async-start | bytes 1880064 | tf_op jit(solution)/shard_map/all_gather | solution.py:48
  160.9 87.3 %copy-start.2 = (bf16[512,384]{1,0:T(8,128)(2,1)S(1)}, bf16[512,384]{1,0:T(8,128)(2,1)}, u32[]{:S(2)}) copy-start(bf16[512,384]{1,0:T(8,128)(2,1)} %param.12) | copy-start | bytes 1179652
  160.9 445.5 %reduce-scatter.5.cloned.1.call-start = ((), (), s32[]{:S(2)}) async-start(), calls=%async_computation.6 | async-start | bytes 2433024 | tf_op jit(solution)/shard_map/reduce_scatter | solution.py:50
  253.9 82.2 %copy-start.1 = (bf16[2304,384]{1,0:T(8,128)(2,1)S(1)}, bf16[2304,384]{1,0:T(8,128)(2,1)}, u32[]{:S(2)}) copy-start(bf16[2304,384]{1,0:T(8,128)(2,1)} %all-gather.8.cloned.1.call-done) | copy-start | bytes 5308420
  339.8 36.6 %copy-start.5 = (bf16[2304,512]{1,0:T(8,128)(2,1)S(1)}, bf16[2304,512]{1,0:T(8,128)(2,1)}, u32[]{:S(2)}) copy-start(bf16[2304,512]{1,0:T(8,128)(2,1)} %all-gather.6.cloned.1.call-done) | copy-start | bytes 7077892
Sparse Core Ops, SparseCore 0:
  11.2 88.7 all-gather.5
  104.5 52.8 reduce-scatter.2
  160.3 44.5 all-gather.7
  207.6 40.5 all-gather.9
  251.7 84.3 all-gather.11
  338.9 37.4 all-gather.13
  382.0 224.4 reduce-scatter.4
where the time goes:
time: 614 us; the launch traced here: 613 us
  waiting for transfers between devices  571 us (93%)
  matrix products  24.6 us (4%)
  between operations  14.2 us (2%)
    reduce_scatter x1, waiting for transfers between devices, local(): lax.psum_scatter((contract_last(gate_grad, w_gate) + contract_last(up_gra...  227 us
    all_gather x1, waiting for transfers between devices, local(): lax.all_gather(out_grad, 'col', axis=0, tiled=True)  92 us
    all_gather x1, waiting for transfers between devices, local(): lax.all_gather(tokens, 'col', axis=0, tiled=True)  82.2 us
    reduce_scatter x1, waiting for transfers between devices, local(): lax.psum_scatter(contract_last(grad_rows, w_down).astype(jnp.bfloat16), '...  53 us
    all_gather x1, waiting for transfers between devices, local(): lax.all_gather(gate_share, 'row', axis=0, tiled=True)  43.9 us
    all_gather x1, waiting for transfers between devices, local(): lax.all_gather(up_share, 'row', axis=0, tiled=True)  38.3 us
    all_gather x1, waiting for transfers between devices, local(): lax.all_gather(hidden_share, 'row', axis=0, tiled=True)  32.2 us
    dot_general x3, matrix products, contract_last(): lax.dot_general(left_side, right_side, (((1,), (1,)), ((), ())), preferre...  15.1 us
  transfers between devices with their start and end apart: 7, of which 7 were waited for; matrix products, arithmetic and copies ran while one was open for 4% of the time, Pallas kernels for 0%

commit v1 on v0

--- a/solution.py
+++ b/solution.py
@@ -43,7 +43,9 @@
     ).astype(jnp.float32)
     gate_share, up_share, hidden_share = swiglu_grads(hidden_grad, gate_pre, up_pre)
     gate_grad, up_grad, hidden = (
-        lax.all_gather(gate_share, "row", axis=0, tiled=True),
+        jnp.concatenate(
+            lax.all_to_all(jnp.stack([gate_share] * lax.axis_size("row")), "row", 0, 0), axis=0
+        ),
         lax.all_gather(up_share, "row", axis=0, tiled=True),
         lax.all_gather(hidden_share, "row", axis=0, tiled=True),
     )

time: 614 us -> 590 us (0.961)
  the two profiles are of different devices: /device:TPU:16 before, /device:TPU:8 now
where the time goes in v1:
time: 590 us
  waiting for transfers between devices  539 us (91%)
  matrix products  23.7 us (4%)
  between operations  14.2 us (2%)
  starting transfers between devices  8.31 us (1%)
    reduce_scatter x1, waiting for transfers between devices, local(): lax.psum_scatter((contract_last(gate_grad, w_gate) + contract_last(up_gra...  225 us
    all_gather x1, waiting for transfers between devices, local(): lax.all_gather(out_grad, 'col', axis=0, tiled=True)  92.1 us
    all_gather x1, waiting for transfers between devices, local(): lax.all_gather(tokens, 'col', axis=0, tiled=True)  84.3 us
    reduce_scatter x1, waiting for transfers between devices, local(): lax.psum_scatter(contract_last(grad_rows, w_down).astype(jnp.bfloat16), '...  55 us
    all_to_all x1, waiting for transfers between devices, local(): lax.all_to_all(jnp.stack([gate_share] * lax.axis_size('row')), 'row', 0, 0)  46.7 us
    all_gather x1, waiting for transfers between devices, local(): lax.all_gather(hidden_share, 'row', axis=0, tiled=True)  33.1 us
    dot_general x3, matrix products, contract_last(): lax.dot_general(left_side, right_side, (((1,), (1,)), ((), ())), preferre...  13.6 us
  transfers between devices with their start and end apart: 7, of which 7 were waited for; matrix products, arithmetic and copies ran while one was open for 4% of the time, Pallas kernels for 0%

profile of v1, /device:TPU:8, one launch (start us, length us, event | category | flops | bytes accessed | tf_op | source)
XLA Modules:
  0.0 590.2 jit_solution(165388246930538357)
XLA Ops:
  7.2 0.0 copy-start
  7.2 0.0 all-gather.5.cloned.1.call-start
  7.2 0.7 all-gather.5.cloned.1.call-update
  7.9 0.0 reduce-scatter.3.cloned.1.call-start
  8.0 92.1 %all-gather.5.cloned.1.call-done = bf16[2304,512]{1,0:T(8,128)(2,1)} async-done(((bf16[72,512]{1,0:T(8,128)(2,1)}), bf16[2304,512]{1,0:T(8,128)(2,1)}) %all-gather.5.cloned.1.call-update) | async-done | bytes 2359312 | tf_op jit(solution)/shard_map/all_gather | solution.py:35
  100.0 4.4 convolution_convert_fusion
  104.4 0.0 reduce-scatter.3.cloned.1.call-update
  104.4 0.0 all-gather.7.cloned.1.call-start
  104.5 55.0 %reduce-scatter.3.cloned.1.call-done = bf16[144,384]{1,0:T(8,128)(2,1)} async-done(((bf16[2304,384]{1,0:T(8,128)(2,1)}), bf16[144,384]{1,0:T(8,128)(2,1)}) %reduce-scatter.3.cloned.1.call-update) | async-done | bytes 110608 | tf_op jit(solution)/shard_map/reduce_scatter | solution.py:38
  159.5 1.7 fusion.10
  161.2 0.0 all-gather.7.cloned.1.call-update
  161.2 0.0 all-gather.9.cloned.1.call-start
  161.2 0.5 all-gather.9.cloned.1.call-update
  161.8 1.4 stack.2
  163.1 8.1 %all-to-all-start = ((bf16[16,144,384]{2,1,0:T(8,128)(2,1)}), bf16[16,144,384]{2,1,0:T(8,128)(2,1)S(1)}, u32[]{:S(2)}, u32[]{:S(2)}) async-start(bf16[16,144,384]{2,1,0:T(8,128)(2,1)} %stack.2), calls=%async_computation.1 | async-start | bytes 3538944 | tf_op jit(solution)/shard_map/all_to_all | solution.py:47
  171.2 0.0 all-gather.11.cloned.1.call-start
  171.3 0.5 all-gather.11.cloned.1.call-update
  171.8 0.0 reduce-scatter.5.cloned.1.call-start
  171.9 46.7 %all-to-all-done = bf16[16,144,384]{2,1,0:T(8,128)(2,1)S(1)} async-done(((bf16[16,144,384]{2,1,0:T(8,128)(2,1)}), bf16[16,144,384]{2,1,0:T(8,128)(2,1)S(1)}, u32[]{:S(2)}, u32[]{:S(2)}) %all-to-all-start) | async-done | bytes 1769504 | tf_op jit(solution)/shard_map/all_to_all | solution.py:47
  218.5 0.0 copy-done
  218.5 3.5 fusion.15
  222.1 1.1 all-gather.7.cloned.1.call-done
  223.2 5.7 fusion
  228.9 0.0 reduce-scatter.5.cloned.1.call-update
  228.9 84.3 %all-gather.9.cloned.1.call-done = bf16[2304,512]{1,0:T(8,128)(2,1)} async-done(((bf16[72,512]{1,0:T(8,128)(2,1)}), bf16[2304,512]{1,0:T(8,128)(2,1)}) %all-gather.9.cloned.1.call-update) | async-done | bytes 2359312 | tf_op jit(solution)/shard_map/all_gather | solution.py:34
  313.2 3.3 fusion.4
  316.5 0.9 copy.12
  317.4 2.8 fusion.5
  320.2 0.9 copy.11
  321.1 33.1 %all-gather.11.cloned.1.call-done = bf16[2304,384]{1,0:T(8,128)(2,1)} async-done(((bf16[144,384]{1,0:T(8,128)(2,1)}), bf16[2304,384]{1,0:T(8,128)(2,1)}) %all-gather.11.cloned.1.call-update) | async-done | bytes 1769488 | tf_op jit(solution)/shard_map/all_gather | solution.py:50
  354.2 4.1 fusion.3
  358.3 225.1 %reduce-scatter.5.cloned.1.call-done = bf16[72,512]{1,0:T(8,128)(2,1)} async-done(((bf16[2304,512]{1,0:T(8,128)(2,1)}), bf16[72,512]{1,0:T(8,128)(2,1)}) %reduce-scatter.5.cloned.1.call-update) | async-done | bytes 73744 | tf_op jit(solution)/shard_map/reduce_scatter | solution.py:52
  (6 shorter events, 0.0 us)
Async XLA Ops:
  7.2 211.4 %copy-start = (bf16[512,384]{1,0:T(8,128)(2,1)S(1)}, bf16[512,384]{1,0:T(8,128)(2,1)}, u32[]{:S(2)}) copy-start(bf16[512,384]{1,0:T(8,128)(2,1)} %param.11) | copy-start | bytes 1179652
  7.2 92.9 %all-gather.5.cloned.1.call-start = ((), (), s32[]{:S(2)}) async-start(), calls=%async_computation.3 | async-start | bytes 2433024 | tf_op jit(solution)/shard_map/all_gather | solution.py:35
  7.9 151.5 %copy-start.2 = (bf16[144,384]{1,0:T(8,128)(2,1)S(1)}, bf16[144,384]{1,0:T(8,128)(2,1)}, u32[]{:S(2)}) copy-start(bf16[144,384]{1,0:T(8,128)(2,1)} %param.10) | copy-start | bytes 331780
  7.9 151.5 %copy-start.3 = (bf16[144,384]{1,0:T(8,128)(2,1)S(1)}, bf16[144,384]{1,0:T(8,128)(2,1)}, u32[]{:S(2)}) copy-start(bf16[144,384]{1,0:T(8,128)(2,1)} %param.9) | copy-start | bytes 331780
  7.9 151.5 %reduce-scatter.3.cloned.1.call-start = ((), (), s32[]{:S(2)}) async-start(), calls=%async_computation.4 | async-start | bytes 1880064 | tf_op jit(solution)/shard_map/reduce_scatter | solution.py:38
  104.4 118.8 %all-gather.7.cloned.1.call-start = ((), (), s32[]{:S(2)}) async-start(), calls=%async_computation.5 | async-start | bytes 1880064 | tf_op jit(solution)/shard_map/all_gather | solution.py:49
  161.2 152.0 %all-gather.9.cloned.1.call-start = ((), (), s32[]{:S(2)}) async-start(), calls=%async_computation.7 | async-start | bytes 2433024 | tf_op jit(solution)/shard_map/all_gather | solution.py:34
  163.1 55.4 %all-to-all-start = ((bf16[16,144,384]{2,1,0:T(8,128)(2,1)}), bf16[16,144,384]{2,1,0:T(8,128)(2,1)S(1)}, u32[]{:S(2)}, u32[]{:S(2)}) async-start(bf16[16,144,384]{2,1,0:T(8,128)(2,1)} %stack.2), calls=%async_computation.1 | async-start | bytes 3538944 | tf_op jit(solution)/shard_map/all_to_all | solution.py:47
  171.2 183.0 %all-gather.11.cloned.1.call-start = ((), (), s32[]{:S(2)}) async-start(), calls=%async_computation.8 | async-start | bytes 1880064 | tf_op jit(solution)/shard_map/all_gather | solution.py:50
  171.8 411.5 %reduce-scatter.5.cloned.1.call-start = ((), (), s32[]{:S(2)}) async-start(), calls=%async_computation.6 | async-start | bytes 2433024 | tf_op jit(solution)/shard_map/reduce_scatter | solution.py:52
  218.5 4.7 copy-start.1
Sparse Core Ops, SparseCore 0:
  11.2 88.8 all-gather.4
  104.6 54.8 reduce-scatter.2
  162.4 60.7 all-gather.6
  226.7 86.4 all-gather.8
  316.0 38.1 all-gather.10
  359.7 223.5 reduce-scatter.4
